TPU v7x, 32 devices: a whole 2x2x4 slice. The times are simulated.
32 devices in a mesh: groups: 2 (over x), blk: 16 (over z, y, core).
Axes of the slice: x: 2, y: 2, z: 4, core: 2. Of those that a mesh axis runs over, the one named last changes fastest.
Arguments:
- vertices: float32 [3, 16384], P(None, ('groups', 'blk')), parts along dimension 1, may hold values from 0 to 1
- source_tri: int32 [3, 32768], P(None, ('groups', 'blk')), parts along dimension 1, may hold values from 0 to 511
- source_disp: float32 [3, 32768], P(None, ('groups', 'blk')), parts along dimension 1, may hold values from -6 to 6
- target_tri: int32 [3, 16384], P(None, ('groups', 'blk')), parts along dimension 1, may hold values from 0 to 511
- fracture_of: int32 [16384], P(('groups', 'blk')), parts along dimension 0, may hold values from 0 to 127
- pressure_coeffs: float32 [4, 256], P(None, ('groups', 'blk')), parts along dimension 1, may hold values from -2 to 2
Outputs:
- force: float32 [3, 16384], P(None, ('groups', 'blk')), parts along dimension 1
There are 2 independent parts, one for each index of `groups`. A program takes and returns all parts, laid end to end along the dimension named above; each array names one. Nothing has to cross between parts.
Inputs may be any that keep to these rules, and one draw needn't show every extreme that they name: `source_tri`: source triangle c uses vertices (c // 1024) * 512 + value. `target_tri`: target triangle c uses vertices (c // 512) * 512 + value.
All inputs are finite; a program needn't handle non-finite values.
Results may differ from a plain program's by a relative error of at most 0.00023.
Values sent between devices are 32-bit elements; how exact they have to be, the bound alone decides.
A program may use at most 64 MiB of HBM per device.

v0:
```python
import math

import jax
import jax.numpy as jnp
from jax import lax
from jax.sharding import PartitionSpec as P

core_sq = 0.01
force_gain = 40.0


def corners(vertices, triangles):
    first = jnp.take(vertices, triangles[0], axis=1)
    second = jnp.take(vertices, triangles[1], axis=1)
    third = jnp.take(vertices, triangles[2], axis=1)
    centers = (first + second + third) / 3.0
    areas = 0.5 * jnp.cross(second - first, third - first, axis=0)
    return (centers, areas)


def pair_forces(points, normals, sources_part):
    centers = sources_part[0:3]
    areas = sources_part[3:6]
    jumps = sources_part[6:9]
    seps = [points[k][:, None] - centers[k][None, :] for k in range(3)]
    dist_sq = seps[0] * seps[0] + seps[1] * seps[1] + seps[2] * seps[2] + core_sq
    inv_dist = lax.rsqrt(dist_sq)
    normal_area = sum((normals[k][:, None] * areas[k][None, :] for k in range(3)))
    sep_jump = sum((seps[k] * jumps[k][None, :] for k in range(3)))
    normal_sep = sum((normals[k][:, None] * seps[k] for k in range(3)))
    coef_one = inv_dist * normal_area
    coef_two = inv_dist * inv_dist * inv_dist * sep_jump * normal_sep
    dims = (((1,), (1,)), ((), ()))
    part_one = lax.dot_general(jumps, coef_one, dims, precision=lax.Precision.HIGHEST)
    part_two = lax.dot_general(areas, coef_two, dims, precision=lax.Precision.HIGHEST)
    return part_one + part_two


def accumulate(points, normals, sources_part):
    width = sources_part.shape[1]
    step_cols = min(width, 2048)
    num_steps = -(-width // step_cols)
    if num_steps == 1:
        return pair_forces(points, normals, sources_part)
    padded = jnp.pad(sources_part, ((0, 0), (0, num_steps * step_cols - width)))
    stacked = padded.reshape(9, num_steps, step_cols).transpose(1, 0, 2)

    def add_step(running, src_step):
        return (running + pair_forces(points, normals, src_step), None)

    start_acc = jnp.zeros((3, points.shape[1]), jnp.float32)
    result, _ = lax.scan(add_step, start_acc, stacked)
    return result


def local(vertices, source_tri, source_disp, target_tri, fracture_of, pressure_coeffs):
    n_devices = lax.axis_size("blk")
    tgt_count = target_tri.shape[1]
    src_centers, src_areas = corners(vertices, source_tri)
    tgt_centers, tgt_normals = corners(vertices, target_tri)
    sources = jnp.concatenate([src_centers, src_areas, source_disp], axis=0)
    gain = force_gain / math.sqrt(source_tri.shape[1] * n_devices)
    start_acc = jnp.zeros((3, tgt_count), jnp.float32)
    influence = start_acc + accumulate(
        tgt_centers, tgt_normals, lax.all_gather(sources, "blk", axis=1, tiled=True)
    )
    all_coeffs = lax.all_gather(pressure_coeffs, "blk", axis=1, tiled=True)
    frac_total = all_coeffs.shape[1]
    one_hot = (jnp.arange(frac_total, dtype=jnp.int32)[:, None] == fracture_of[None, :]).astype(
        jnp.float32
    )
    picked = jnp.dot(all_coeffs, one_hot, precision=lax.Precision.HIGHEST)
    pressure = (
        picked[0]
        + picked[1] * tgt_centers[0]
        + picked[2] * tgt_centers[1]
        + picked[3] * tgt_centers[2]
    )
    return gain * influence - pressure[None, :] * tgt_normals


def solution(mesh):
    in_specs = (
        P(None, ("groups", "blk")),
        P(None, ("groups", "blk")),
        P(None, ("groups", "blk")),
        P(None, ("groups", "blk")),
        P(("groups", "blk")),
        P(None, ("groups", "blk")),
    )
    out_specs = P(None, ("groups", "blk"))
    return jax.shard_map(local, mesh=mesh, in_specs=in_specs, out_specs=out_specs, check_vma=False)
```

profile of v0, /device:TPU:0, one launch (start us, length us, event | category | flops | bytes accessed | tf_op | source)
XLA Modules:
  0.0 158.2 jit_solution(12911403741173008262)
XLA Ops:
  1.7 1.0 gather_fusion.3
  2.9 1.0 gather_fusion.4
  5.4 2.8 %gather_fusion = f32[1024,3]{1,0:T(8,128)S(1)} fusion(f32[3,512]{0,1:T(8,128)S(1)} %copy.56, s32[1024]{0:T(1024)S(1)} %fusion.67), kind=kCustom, calls=%fused_computation.clone | custom fusion | bytes 28672 | tf_op jit(solution)/shard_map/jit(_take)/gather | solution.py:13
  8.4 2.8 %gather_fusion.1 = f32[1024,3]{1,0:T(8,128)S(1)} fusion(f32[3,512]{0,1:T(8,128)S(1)} %copy.56, s32[1024]{0:T(1024)S(1)} %fusion.68), kind=kCustom, calls=%fused_computation.2.clone | custom fusion | bytes 28672 | tf_op jit(solution)/shard_map/jit(_take)/gather | solution.py:14
  11.4 2.8 %gather_fusion.2 = f32[1024,3]{1,0:T(8,128)S(1)} fusion(f32[3,512]{0,1:T(8,128)S(1)} %copy.56, s32[1024]{0:T(1024)S(1)} %fusion.69), kind=kCustom, calls=%fused_computation.3.clone | custom fusion | bytes 28672 | tf_op jit(solution)/shard_map/jit(_take)/gather | solution.py:15
  14.6 26.2 %all_gather.6 = f32[9,16384]{1,0:T(8,128)S(1)} all-gather(f32[9,1024]{1,0:T(8,128)S(1)} %pad_maximum_fusion), channel_id=1, replica_groups=mesh['groups'=2,'blk'=16] {'blk'}, dimensions={1}, use_global_device_ids=true | all-gather | bytes 626688 | tf_op jit(solution)/shard_map/all_gather | solution.py:65
  41.9 97.9 %while.11 = (s32[]{:T(128)}, f32[3,512]{1,0:T(4,128)S(1)}, f32[8,9,2048]{2,1,0:T(8,128)S(1)}, f32[3,512]{1,0:T(4,128)S(1)}, f32[3,512]{1,0:T(4,128)S(1)}, /*inde...) while((s32[]{:T(128)}, f32[3,512]{1,0:T(4,128)S(1)}, ...), condition=%wide.region_1.4_spmd.clone, body=%wide.region_0.3_spmd.clone.sunk | while | flops 115347976 | bytes 389419 | solution.py:52
  42.2 6.6 %fusion.87 = f32[3,512]{1,0:T(4,128)S(1)} fusion(f32[2048]{0:T(1024)S(1)} %bitcast.146, f32[2048]{0:T(1024)S(1)} %bitcast.144, f32[2048]{0:T(1024)S(1)} %bitcast.145, f32[512]{0:T(512)S(1)} %bitcast.155, f32[512]{0:T(512)S(1)} %bitcast.153, f32[512]{0:T(512)S(1)} %bitcast.157, f32[2048]{0:T(1024)S(1)} %bitcast.138, f32[512]{0:T(512)S(1)} %bitcast.149, ...), kind=kOutput, calls=%fused_computation.18.clone.1 | convolution fusion | flops 61865984 | bytes 100360 | tf_op jit(solution)/shard_map/while/body/eval_jaxpr/dot_general | solution.py:35
  48.7 5.5 %fusion.88 = f32[3,512]{1,0:T(4,128)S(1)} fusion(f32[3,512]{1,0:T(4,128)S(1)} %fusion.87, f32[2048]{0:T(1024)S(1)} %bitcast.136, f32[512]{0:T(512)S(1)} %bitcast.156, f32[2048]{0:T(1024)S(1)} %bitcast.137, f32[512]{0:T(512)S(1)} %bitcast.154, f32[2048]{0:T(1024)S(1)} %bitcast.135, f32[512]{0:T(512)S(1)} %bitcast.158, f32[2048]{0:T(1024)S(1)} %bitcast.139, ...), kind=kOutput, calls=%fused_computation.61.clone.1 | convolution fusion | flops 53481984 | bytes 116745 | tf_op jit(solution)/shard_map/while/body/eval_jaxpr/dot_general | solution.py:34
  54.4 6.6 %fusion.87 = f32[3,512]{1,0:T(4,128)S(1)} fusion(f32[2048]{0:T(1024)S(1)} %bitcast.146, f32[2048]{0:T(1024)S(1)} %bitcast.144, f32[2048]{0:T(1024)S(1)} %bitcast.145, f32[512]{0:T(512)S(1)} %bitcast.155, f32[512]{0:T(512)S(1)} %bitcast.153, f32[512]{0:T(512)S(1)} %bitcast.157, f32[2048]{0:T(1024)S(1)} %bitcast.138, f32[512]{0:T(512)S(1)} %bitcast.149, ...), kind=kOutput, calls=%fused_computation.18.clone.1 | convolution fusion | flops 61865984 | bytes 100360 | tf_op jit(solution)/shard_map/while/body/eval_jaxpr/dot_general | solution.py:35
  61.0 5.5 %fusion.88 = f32[3,512]{1,0:T(4,128)S(1)} fusion(f32[3,512]{1,0:T(4,128)S(1)} %fusion.87, f32[2048]{0:T(1024)S(1)} %bitcast.136, f32[512]{0:T(512)S(1)} %bitcast.156, f32[2048]{0:T(1024)S(1)} %bitcast.137, f32[512]{0:T(512)S(1)} %bitcast.154, f32[2048]{0:T(1024)S(1)} %bitcast.135, f32[512]{0:T(512)S(1)} %bitcast.158, f32[2048]{0:T(1024)S(1)} %bitcast.139, ...), kind=kOutput, calls=%fused_computation.61.clone.1 | convolution fusion | flops 53481984 | bytes 116745 | tf_op jit(solution)/shard_map/while/body/eval_jaxpr/dot_general | solution.py:34
  66.6 6.6 %fusion.87 = f32[3,512]{1,0:T(4,128)S(1)} fusion(f32[2048]{0:T(1024)S(1)} %bitcast.146, f32[2048]{0:T(1024)S(1)} %bitcast.144, f32[2048]{0:T(1024)S(1)} %bitcast.145, f32[512]{0:T(512)S(1)} %bitcast.155, f32[512]{0:T(512)S(1)} %bitcast.153, f32[512]{0:T(512)S(1)} %bitcast.157, f32[2048]{0:T(1024)S(1)} %bitcast.138, f32[512]{0:T(512)S(1)} %bitcast.149, ...), kind=kOutput, calls=%fused_computation.18.clone.1 | convolution fusion | flops 61865984 | bytes 100360 | tf_op jit(solution)/shard_map/while/body/eval_jaxpr/dot_general | solution.py:35
  73.2 5.5 %fusion.88 = f32[3,512]{1,0:T(4,128)S(1)} fusion(f32[3,512]{1,0:T(4,128)S(1)} %fusion.87, f32[2048]{0:T(1024)S(1)} %bitcast.136, f32[512]{0:T(512)S(1)} %bitcast.156, f32[2048]{0:T(1024)S(1)} %bitcast.137, f32[512]{0:T(512)S(1)} %bitcast.154, f32[2048]{0:T(1024)S(1)} %bitcast.135, f32[512]{0:T(512)S(1)} %bitcast.158, f32[2048]{0:T(1024)S(1)} %bitcast.139, ...), kind=kOutput, calls=%fused_computation.61.clone.1 | convolution fusion | flops 53481984 | bytes 116745 | tf_op jit(solution)/shard_map/while/body/eval_jaxpr/dot_general | solution.py:34
  78.8 6.6 %fusion.87 = f32[3,512]{1,0:T(4,128)S(1)} fusion(f32[2048]{0:T(1024)S(1)} %bitcast.146, f32[2048]{0:T(1024)S(1)} %bitcast.144, f32[2048]{0:T(1024)S(1)} %bitcast.145, f32[512]{0:T(512)S(1)} %bitcast.155, f32[512]{0:T(512)S(1)} %bitcast.153, f32[512]{0:T(512)S(1)} %bitcast.157, f32[2048]{0:T(1024)S(1)} %bitcast.138, f32[512]{0:T(512)S(1)} %bitcast.149, ...), kind=kOutput, calls=%fused_computation.18.clone.1 | convolution fusion | flops 61865984 | bytes 100360 | tf_op jit(solution)/shard_map/while/body/eval_jaxpr/dot_general | solution.py:35
  85.4 5.5 %fusion.88 = f32[3,512]{1,0:T(4,128)S(1)} fusion(f32[3,512]{1,0:T(4,128)S(1)} %fusion.87, f32[2048]{0:T(1024)S(1)} %bitcast.136, f32[512]{0:T(512)S(1)} %bitcast.156, f32[2048]{0:T(1024)S(1)} %bitcast.137, f32[512]{0:T(512)S(1)} %bitcast.154, f32[2048]{0:T(1024)S(1)} %bitcast.135, f32[512]{0:T(512)S(1)} %bitcast.158, f32[2048]{0:T(1024)S(1)} %bitcast.139, ...), kind=kOutput, calls=%fused_computation.61.clone.1 | convolution fusion | flops 53481984 | bytes 116745 | tf_op jit(solution)/shard_map/while/body/eval_jaxpr/dot_general | solution.py:34
  91.0 6.6 %fusion.87 = f32[3,512]{1,0:T(4,128)S(1)} fusion(f32[2048]{0:T(1024)S(1)} %bitcast.146, f32[2048]{0:T(1024)S(1)} %bitcast.144, f32[2048]{0:T(1024)S(1)} %bitcast.145, f32[512]{0:T(512)S(1)} %bitcast.155, f32[512]{0:T(512)S(1)} %bitcast.153, f32[512]{0:T(512)S(1)} %bitcast.157, f32[2048]{0:T(1024)S(1)} %bitcast.138, f32[512]{0:T(512)S(1)} %bitcast.149, ...), kind=kOutput, calls=%fused_computation.18.clone.1 | convolution fusion | flops 61865984 | bytes 100360 | tf_op jit(solution)/shard_map/while/body/eval_jaxpr/dot_general | solution.py:35
  97.6 5.5 %fusion.88 = f32[3,512]{1,0:T(4,128)S(1)} fusion(f32[3,512]{1,0:T(4,128)S(1)} %fusion.87, f32[2048]{0:T(1024)S(1)} %bitcast.136, f32[512]{0:T(512)S(1)} %bitcast.156, f32[2048]{0:T(1024)S(1)} %bitcast.137, f32[512]{0:T(512)S(1)} %bitcast.154, f32[2048]{0:T(1024)S(1)} %bitcast.135, f32[512]{0:T(512)S(1)} %bitcast.158, f32[2048]{0:T(1024)S(1)} %bitcast.139, ...), kind=kOutput, calls=%fused_computation.61.clone.1 | convolution fusion | flops 53481984 | bytes 116745 | tf_op jit(solution)/shard_map/while/body/eval_jaxpr/dot_general | solution.py:34
  103.2 6.6 %fusion.87 = f32[3,512]{1,0:T(4,128)S(1)} fusion(f32[2048]{0:T(1024)S(1)} %bitcast.146, f32[2048]{0:T(1024)S(1)} %bitcast.144, f32[2048]{0:T(1024)S(1)} %bitcast.145, f32[512]{0:T(512)S(1)} %bitcast.155, f32[512]{0:T(512)S(1)} %bitcast.153, f32[512]{0:T(512)S(1)} %bitcast.157, f32[2048]{0:T(1024)S(1)} %bitcast.138, f32[512]{0:T(512)S(1)} %bitcast.149, ...), kind=kOutput, calls=%fused_computation.18.clone.1 | convolution fusion | flops 61865984 | bytes 100360 | tf_op jit(solution)/shard_map/while/body/eval_jaxpr/dot_general | solution.py:35
  109.8 5.5 %fusion.88 = f32[3,512]{1,0:T(4,128)S(1)} fusion(f32[3,512]{1,0:T(4,128)S(1)} %fusion.87, f32[2048]{0:T(1024)S(1)} %bitcast.136, f32[512]{0:T(512)S(1)} %bitcast.156, f32[2048]{0:T(1024)S(1)} %bitcast.137, f32[512]{0:T(512)S(1)} %bitcast.154, f32[2048]{0:T(1024)S(1)} %bitcast.135, f32[512]{0:T(512)S(1)} %bitcast.158, f32[2048]{0:T(1024)S(1)} %bitcast.139, ...), kind=kOutput, calls=%fused_computation.61.clone.1 | convolution fusion | flops 53481984 | bytes 116745 | tf_op jit(solution)/shard_map/while/body/eval_jaxpr/dot_general | solution.py:34
  115.4 6.6 %fusion.87 = f32[3,512]{1,0:T(4,128)S(1)} fusion(f32[2048]{0:T(1024)S(1)} %bitcast.146, f32[2048]{0:T(1024)S(1)} %bitcast.144, f32[2048]{0:T(1024)S(1)} %bitcast.145, f32[512]{0:T(512)S(1)} %bitcast.155, f32[512]{0:T(512)S(1)} %bitcast.153, f32[512]{0:T(512)S(1)} %bitcast.157, f32[2048]{0:T(1024)S(1)} %bitcast.138, f32[512]{0:T(512)S(1)} %bitcast.149, ...), kind=kOutput, calls=%fused_computation.18.clone.1 | convolution fusion | flops 61865984 | bytes 100360 | tf_op jit(solution)/shard_map/while/body/eval_jaxpr/dot_general | solution.py:35
  122.0 5.5 %fusion.88 = f32[3,512]{1,0:T(4,128)S(1)} fusion(f32[3,512]{1,0:T(4,128)S(1)} %fusion.87, f32[2048]{0:T(1024)S(1)} %bitcast.136, f32[512]{0:T(512)S(1)} %bitcast.156, f32[2048]{0:T(1024)S(1)} %bitcast.137, f32[512]{0:T(512)S(1)} %bitcast.154, f32[2048]{0:T(1024)S(1)} %bitcast.135, f32[512]{0:T(512)S(1)} %bitcast.158, f32[2048]{0:T(1024)S(1)} %bitcast.139, ...), kind=kOutput, calls=%fused_computation.61.clone.1 | convolution fusion | flops 53481984 | bytes 116745 | tf_op jit(solution)/shard_map/while/body/eval_jaxpr/dot_general | solution.py:34
  127.6 6.6 %fusion.87 = f32[3,512]{1,0:T(4,128)S(1)} fusion(f32[2048]{0:T(1024)S(1)} %bitcast.146, f32[2048]{0:T(1024)S(1)} %bitcast.144, f32[2048]{0:T(1024)S(1)} %bitcast.145, f32[512]{0:T(512)S(1)} %bitcast.155, f32[512]{0:T(512)S(1)} %bitcast.153, f32[512]{0:T(512)S(1)} %bitcast.157, f32[2048]{0:T(1024)S(1)} %bitcast.138, f32[512]{0:T(512)S(1)} %bitcast.149, ...), kind=kOutput, calls=%fused_computation.18.clone.1 | convolution fusion | flops 61865984 | bytes 100360 | tf_op jit(solution)/shard_map/while/body/eval_jaxpr/dot_general | solution.py:35
  134.2 5.5 %fusion.88 = f32[3,512]{1,0:T(4,128)S(1)} fusion(f32[3,512]{1,0:T(4,128)S(1)} %fusion.87, f32[2048]{0:T(1024)S(1)} %bitcast.136, f32[512]{0:T(512)S(1)} %bitcast.156, f32[2048]{0:T(1024)S(1)} %bitcast.137, f32[512]{0:T(512)S(1)} %bitcast.154, f32[2048]{0:T(1024)S(1)} %bitcast.135, f32[512]{0:T(512)S(1)} %bitcast.158, f32[2048]{0:T(1024)S(1)} %bitcast.139, ...), kind=kOutput, calls=%fused_computation.61.clone.1 | convolution fusion | flops 53481984 | bytes 116745 | tf_op jit(solution)/shard_map/while/body/eval_jaxpr/dot_general | solution.py:34
  139.8 17.5 %all-gather = f32[16,8,4]{1,2,0:T(4,128)S(1)} all-gather(f32[1,8,4]{1,2,0:T(4,128)S(1)} %bitcast.172), channel_id=1, replica_groups=mesh['groups'=2,'blk'=16] {'blk'}, dimensions={0}, use_global_device_ids=true | all-gather | bytes 2176 | tf_op jit(solution)/shard_map/all_gather | solution.py:67
  (63 shorter events, 6.5 us)
Async XLA Ops:
  0.0 5.3 %copy-start.1 = (s32[3,1024]{1,0:T(4,128)S(1)}, s32[3,1024]{1,0:T(4,128)}, u32[]{:S(2)}) copy-start(s32[3,1024]{1,0:T(4,128)} %param.13) | copy-start | bytes 36868
  8.2 6.4 %copy-start = (f32[3,1024]{1,0:T(4,128)S(1)}, f32[3,1024]{1,0:T(4,128)}, u32[]{:S(2)}) copy-start(f32[3,1024]{1,0:T(4,128)} %param.14) | copy-start | bytes 36868
  41.9 97.9 %copy-start.2 = (f32[4,8]{1,0:T(4,128)S(1)}, f32[4,8]{1,0:T(4,128)}, u32[]{:S(2)}) copy-start(f32[4,8]{1,0:T(4,128)} %param.17) | copy-start | bytes 388
  41.9 115.5 %copy-start.3 = (s32[512]{0:T(512)S(1)}, s32[512]{0:T(512)}, u32[]{:S(2)}) copy-start(s32[512]{0:T(512)} %param.16) | copy-start | bytes 6148
where the time goes:
time: 159 us; the launch traced here: 158 us
  matrix products  96.9 us (61%)
  blocking collectives  43.8 us (28%)
  local copies, waits for them, and re-layouts  15.9 us (10%)
    dot_general x8, matrix products, pair_forces(): lax.dot_general(areas, coef_two, dims, precision=lax.Precision.HIGHEST)  52.5 us
    dot_general x8, matrix products, pair_forces(): lax.dot_general(jumps, coef_one, dims, precision=lax.Precision.HIGHEST)  44.2 us
    all_gather x1, blocking collectives, local(): lax.all_gather(sources, 'blk', axis=1, tiled=True)  26.2 us
    all_gather x1, blocking collectives, local(): all_coeffs = lax.all_gather(pressure_coeffs, 'blk', axis=1, tiled=True)  17.5 us
    gather x4, local copies, waits for them, and re-layouts, corners(): second = jnp.take(vertices, triangles[1], axis=1)  4.15 us
    gather x4, local copies, waits for them, and re-layouts, corners(): third = jnp.take(vertices, triangles[2], axis=1)  4.15 us
    gather x4, local copies, waits for them, and re-layouts, corners(): first = jnp.take(vertices, triangles[0], axis=1)  4.14 us

commit v1 on v0

v1 whole, which is shorter than its diff:
```python
import functools
import math

import jax
import jax.numpy as jnp
from jax import lax
from jax.experimental import pallas as pl
from jax.experimental.pallas import tpu as pltpu
from jax.sharding import PartitionSpec as P

core_sq = 0.01
force_gain = 40.0
LANES = 128
PIECES = 3
GROUP = 2
f32 = jnp.float32
bf16 = jnp.bfloat16


def split(value, pieces):
    out = []
    for _ in range(pieces):
        piece = value.astype(bf16).astype(f32)
        out.append(piece)
        value = value - piece
    return out


def lookup(table, index):
    columns = []
    for t in range(index.shape[1] // LANES):
        where = index[:, t * LANES : (t + 1) * LANES]
        low, high = where % LANES, where // LANES
        got = None
        for c in range(table.shape[1] // LANES):
            part = jnp.broadcast_to(table[:, c * LANES : (c + 1) * LANES], (8, LANES))
            part = jnp.take_along_axis(part, low, axis=1, mode="promise_in_bounds")
            got = part if got is None else jnp.where(high == c, part, got)
        columns.append(got)
    return jnp.concatenate(columns, axis=1)


def triangles(corner, first):
    p0, p1, p2 = ([corner[k][first + c : first + c + 1] for k in range(3)] for c in range(3))
    centers = [(p0[k] + p1[k] + p2[k]) / 3.0 for k in range(3)]
    u = [p1[k] - p0[k] for k in range(3)]
    v = [p2[k] - p0[k] for k in range(3)]
    areas = [0.5 * (u[(k + 1) % 3] * v[(k + 2) % 3] - u[(k + 2) % 3] * v[(k + 1) % 3]) for k in range(3)]
    return centers, areas


def source_features(block, width):
    main = block[:, :width]
    row = lax.broadcasted_iota(jnp.int32, (8, width), 0)
    y = [main[k : k + 1] for k in range(3)]
    a = [main[3 + k : 4 + k] for k in range(3)]
    d = [main[6:7], main[7:8]]
    d.append(
        jnp.concatenate([block[t : t + 1, width : width + LANES] for t in range(width // LANES)], axis=1)
    )
    m1, m2, m3 = split(main, 3)
    q1, q2, q3 = split(main * main, 3)
    ones = jnp.ones((8, width), f32)
    near = jnp.concatenate([m1, m1, m1, m2, m2, m3, q1, q2, q3, ones], axis=0).astype(bf16)
    outer = lambda t: jnp.where(row < 3, t[0], jnp.where(row < 6, t[1], t[2]))
    inner = lambda t: jnp.where(row % 3 == 0, t[0], jnp.where(row % 3 == 1, t[1], t[2]))
    yy = y[0] * y[0] + y[1] * y[1] + y[2] * y[2] + core_sq
    yd = y[0] * d[0] + y[1] * d[1] + y[2] * d[2]
    q = outer(a) * inner(d)
    last = a[2] * d[2]
    last_c = yy * last + y[2] * yd * a[2]
    tiles = [q, y[0] * q, y[1] * q, y[2] * q, yy * q + (yd * outer(y)) * inner(a)]
    tail = jnp.where(row == 0, last, 0.0)
    for k in range(3):
        tail = jnp.where(row == k + 1, y[k] * last, tail)
    tail = jnp.where(row == 4, last_c, tail)
    weights = split(jnp.concatenate(tiles + [tail], axis=0), PIECES)
    return near, jnp.concatenate(weights, axis=0).astype(bf16)


def target_features(x):
    width = x[0].shape[1]
    row = lax.broadcasted_iota(jnp.int32, (8, width), 0)
    coords = jnp.where(row == 0, x[0], jnp.where(row == 1, x[1], jnp.where(row == 2, x[2], 0.0)))
    x1, x2, x3 = split(-2.0 * coords, 3)
    square = x[0] * x[0] + x[1] * x[1] + x[2] * x[2] + core_sq
    s1, s2, s3 = split(square, 3)
    const = jnp.where(row == 0, s1, jnp.where(row == 1, s2, jnp.where(row == 2, s3, 0.0)))
    first3 = jnp.where(row < 3, 1.0, 0.0)
    return jnp.concatenate([x1, x2, x3, x1, x2, x1, first3, first3, first3, const], axis=0).astype(bf16)


def combine(sums, x, n):
    def pick(tile, k, m):
        r = 3 * k + m
        at = 8 * tile + r if r < 8 else 40 + tile
        return sums[at : at + 1]

    first = [[pick(0, k, m) for m in range(3)] for k in range(3)]
    moved = [[[pick(1 + p, k, m) for m in range(3)] for k in range(3)] for p in range(3)]
    const = [[pick(4, k, m) for m in range(3)] for k in range(3)]
    xx = x[0] * x[0] + x[1] * x[1] + x[2] * x[2]
    nx = n[0] * x[0] + n[1] * x[1] + n[2] * x[2]
    rows = []
    for m in range(3):
        total = 0.0
        for k in range(3):
            inside = xx * first[k][m] + const[k][m]
            for p in range(3):
                inside = inside - x[p] * (2.0 * moved[p][k][m] + moved[k][m][p])
            total = total + n[k] * inside
            total = total + nx * (x[k] * first[m][k] - moved[k][m][k])
        rows.append(total)
    return rows


def kernel(
    n_dev, vert_ref, stri_ref, disp_ref, ttri_ref, frac_ref, coef_ref, out_ref,
    held, index, coef, near_t, sums, send_sem, recv_sem,
):
    me = lax.axis_index("blk")
    width = stri_ref.shape[1]
    targets = ttri_ref.shape[1]
    per_dev = coef_ref.shape[1]
    chips = n_dev // 2

    def partner(step, sign):
        chip = lax.rem(me // 2 + sign * (step // 2) + chips, chips)
        return chip * 2 + lax.rem(me + step, 2)

    barrier = pltpu.get_barrier_semaphore()

    def greet(step, _):
        pl.semaphore_signal(
            barrier, inc=1, device_id={"blk": partner(step, 1)}, device_id_type=pl.DeviceIdType.MESH
        )
        return 0

    lax.fori_loop(1, n_dev, greet, 0)

    index[...] = jnp.zeros_like(index)
    index[0:3, :] = stri_ref[...]
    index[3:6, 0:targets] = ttri_ref[...]
    spots = index[...]
    corner = [lookup(vert_ref[k : k + 1, :], spots) for k in range(3)]
    centers, areas = triangles(corner, 0)
    row = lax.broadcasted_iota(jnp.int32, (8, width), 0)
    main = disp_ref[1:2, :]
    for r, value in enumerate([c - 0.5 for c in centers] + areas + [disp_ref[0:1, :]]):
        main = jnp.where(row == r, value, main)
    lane = lax.broadcasted_iota(jnp.int32, (8, LANES), 1)
    coef[...] = jnp.zeros_like(coef)
    coef[0:4, 0:per_dev] = coef_ref[...]
    spread = jnp.take_along_axis(coef[...], lane % per_dev, axis=1, mode="promise_in_bounds")
    per_tile = LANES // per_dev
    spread = jnp.where(lane // per_dev == lax.rem(me, per_tile), spread, 0.0)
    held[me, :, 0:width] = main
    for t in range(width // LANES):
        held[me, t : t + 1, width : width + LANES] = disp_ref[2:3, t * LANES : (t + 1) * LANES]
    held[me, :, width + LANES : width + 2 * LANES] = spread

    def copy(step):
        return pltpu.make_async_remote_copy(
            src_ref=held.at[me],
            dst_ref=held.at[me],
            send_sem=send_sem.at[step],
            recv_sem=recv_sem.at[me],
            device_id={"blk": partner(step, 1)},
            device_id_type=pl.DeviceIdType.MESH,
        )

    def arrived(step):
        source = partner(step, -1)
        pltpu.make_async_remote_copy(
            src_ref=held.at[source],
            dst_ref=held.at[source],
            send_sem=send_sem.at[step],
            recv_sem=recv_sem.at[source],
            device_id={"blk": source},
            device_id_type=pl.DeviceIdType.MESH,
        ).wait_recv()
        return source

    pl.semaphore_wait(barrier, n_dev - 1)

    def send(step, _):
        copy(step).start()
        return 0

    lax.fori_loop(1, n_dev, send, 0)

    corner = [c[:, 0:targets] for c in corner]
    points, normals = triangles(corner, 3)
    x = [p - 0.5 for p in points]
    near_t[...] = target_features(x)
    sums[...] = jnp.zeros_like(sums)

    def add_blocks(sources):
        left, right = [], []
        for source in sources:
            near, weights = source_features(held[source], width)
            dist_sq = lax.dot_general(
                near, near_t[...], (((0,), (0,)), ((), ())), preferred_element_type=f32
            )
            inv = lax.rsqrt(dist_sq)
            cube = inv * inv * inv
            high = cube.astype(bf16)
            low = (cube - high.astype(f32)).astype(bf16)
            left += [weights, weights]
            right += [high, low]
        sums[...] += jnp.dot(
            jnp.concatenate(left, axis=1), jnp.concatenate(right, axis=0), preferred_element_type=f32
        )

    arrived(1)
    add_blocks([me, partner(1, -1)])

    def step_blocks(step, _):
        add_blocks([arrived(GROUP * step + g) for g in range(GROUP)])
        return 0

    lax.fori_loop(1, n_dev // GROUP, step_blocks, 0)

    total = sums[0:48, :]
    for piece in range(1, PIECES):
        total = total + sums[48 * piece : 48 * piece + 48, :]
    influence = combine(total, x, normals)

    tables = -(-n_dev * per_dev // LANES)
    which = jnp.broadcast_to(frac_ref[...], (8, targets))
    low, high = which % LANES, which // LANES
    picked = jnp.zeros((8, targets), f32)
    for g in range(tables):
        table = jnp.zeros((8, LANES), f32)
        for s in range(g * per_tile, min((g + 1) * per_tile, n_dev)):
            table = table + held[s, :, width + LANES : width + 2 * LANES]
        got = jnp.concatenate(
            [
                jnp.take_along_axis(
                    table, low[:, t * LANES : (t + 1) * LANES], axis=1, mode="promise_in_bounds"
                )
                for t in range(targets // LANES)
            ],
            axis=1,
        )
        picked = jnp.where(high == g, got, picked)
    pressure = picked[0:1]
    for k in range(3):
        pressure = pressure + picked[k + 1 : k + 2] * points[k]
    gain = force_gain / math.sqrt(width * n_dev)
    for m in range(3):
        out_ref[m : m + 1, :] = gain * influence[m] - pressure * normals[m]

    def sent(step, _):
        copy(step).wait_send()
        return 0

    lax.fori_loop(1, n_dev, sent, 0)


def solution(mesh):
    n_dev = mesh.shape["blk"]

    def local(vertices, source_tri, source_disp, target_tri, fracture_of, pressure_coeffs):
        width, targets = source_tri.shape[1], target_tri.shape[1]
        vmem = pl.BlockSpec(memory_space=pltpu.VMEM)
        return pl.pallas_call(
            functools.partial(kernel, n_dev),
            out_shape=jax.ShapeDtypeStruct((3, targets), f32),
            in_specs=[vmem] * 6,
            out_specs=vmem,
            scratch_shapes=[
                pltpu.VMEM((n_dev, 8, width + 2 * LANES), f32),
                pltpu.VMEM((8, width), jnp.int32),
                pltpu.VMEM((8, LANES), f32),
                pltpu.VMEM((80, targets), bf16),
                pltpu.VMEM((48 * PIECES, targets), f32),
                pltpu.SemaphoreType.DMA((n_dev,)),
                pltpu.SemaphoreType.DMA((n_dev,)),
            ],
            compiler_params=pltpu.CompilerParams(
                collective_id=0, has_side_effects=True, vmem_limit_bytes=48 << 20
            ),
        )(vertices, source_tri, source_disp, target_tri, fracture_of[None, :], pressure_coeffs)

    both = ("groups", "blk")
    wide = P(None, both)
    return jax.shard_map(
        local, mesh=mesh, in_specs=(wide, wide, wide, wide, P(both), wide), out_specs=wide, check_vma=False
    )
```

time: 159 us -> 31.7 us (0.20)
  the two profiles are of different devices: /device:TPU:0 before, /device:TPU:27 now
where the time goes in v1:
time: 31.7 us; the launch traced here: 31.2 us
  Pallas kernels  26.4 us (83%)
  local copies, waits for them, and re-layouts  4.79 us (15%)
    pallas_call x1, Pallas kernels, local(): pl.pallas_call(functools.partial(kernel, n_dev), out_shape=jax.ShapeDtype...  26.4 us
    unnamed x13, local copies, waits for them, and re-layouts  4.79 us

profile of v1, /device:TPU:27, one launch (start us, length us, event | category | flops | bytes accessed | tf_op | source)
XLA Modules:
  0.0 31.2 jit_solution(14494725992292714697)
XLA Ops:
  0.0 0.0 copy-start
  0.0 0.7 %copy-done = s32[3,1024]{1,0:T(4,128)S(1)} copy-done((s32[3,1024]{1,0:T(4,128)S(1)}, s32[3,1024]{1,0:T(4,128)}, u32[]{:S(2)}) %copy-start) | copy-done | bytes 12312
  0.7 0.0 copy-start.1
  0.7 0.7 %copy-done.1 = f32[3,1024]{1,0:T(4,128)S(1)} copy-done((f32[3,1024]{1,0:T(4,128)S(1)}, f32[3,1024]{1,0:T(4,128)}, u32[]{:S(2)}) %copy-start.1) | copy-done | bytes 12312
  1.4 0.0 copy-start.2
  1.4 0.7 %copy-done.2 = f32[3,512]{1,0:T(4,128)S(1)} copy-done((f32[3,512]{1,0:T(4,128)S(1)}, f32[3,512]{1,0:T(4,128)}, u32[]{:S(2)}) %copy-start.2) | copy-done | bytes 6168
  2.1 0.0 copy-start.3
  2.1 0.7 %copy-done.3 = s32[3,512]{1,0:T(4,128)S(1)} copy-done((s32[3,512]{1,0:T(4,128)S(1)}, s32[3,512]{1,0:T(4,128)}, u32[]{:S(2)}) %copy-start.3) | copy-done | bytes 6168
  2.8 0.0 copy-start.4
  2.8 0.7 %copy-done.4 = s32[512]{0:T(512)S(1)} copy-done((s32[512]{0:T(512)S(1)}, s32[512]{0:T(512)}, u32[]{:S(2)}) %copy-start.4) | copy-done | bytes 2072
  3.5 0.0 copy-start.5
  3.5 0.7 %copy-done.5 = f32[4,8]{1,0:T(4,128)S(1)} copy-done((f32[4,8]{1,0:T(4,128)S(1)}, f32[4,8]{1,0:T(4,128)}, u32[]{:S(2)}) %copy-start.5) | copy-done | bytes 152
  4.2 26.4 %shard_map.64 = f32[3,512]{1,0:T(4,128)S(1)} custom-call(f32[3,512]{1,0:T(4,128)S(1)} %copy-done.2, s32[3,1024]{1,0:T(4,128)S(1)} %copy-done, f32[3,1024]{1,0:T(4,128)S(1)} %copy-done.1, s32[3,512]{1,0:T(4,128)S(1)} %copy-done.3, s32[1,512]{1,0:T(1,128)S(1)} %bitcast.1, f32[4,8]{1,0:T(4,128)S(1)} %copy-done.5), custom_call_target="tpu_custom_call" | custom-call | tf_op jit(solution)/shard_map/pallas_call | solution.py:267
  30.6 0.6 %copy.8 = f32[3,512]{1,0:T(4,128)} copy(f32[3,512]{1,0:T(4,128)S(1)} %shard_map.64) | data formatting | bytes 12288
Async XLA Ops:
  0.0 0.7 %copy-start = (s32[3,1024]{1,0:T(4,128)S(1)}, s32[3,1024]{1,0:T(4,128)}, u32[]{:S(2)}) copy-start(s32[3,1024]{1,0:T(4,128)} %stri_ref.1) | copy-start | bytes 36868
  0.7 0.7 %copy-start.1 = (f32[3,1024]{1,0:T(4,128)S(1)}, f32[3,1024]{1,0:T(4,128)}, u32[]{:S(2)}) copy-start(f32[3,1024]{1,0:T(4,128)} %disp_ref.1) | copy-start | bytes 36868
  1.4 0.7 %copy-start.2 = (f32[3,512]{1,0:T(4,128)S(1)}, f32[3,512]{1,0:T(4,128)}, u32[]{:S(2)}) copy-start(f32[3,512]{1,0:T(4,128)} %vert_ref.1) | copy-start | bytes 18436
  2.1 0.7 %copy-start.3 = (s32[3,512]{1,0:T(4,128)S(1)}, s32[3,512]{1,0:T(4,128)}, u32[]{:S(2)}) copy-start(s32[3,512]{1,0:T(4,128)} %ttri_ref.1) | copy-start | bytes 18436
  2.8 0.7 %copy-start.4 = (s32[512]{0:T(512)S(1)}, s32[512]{0:T(512)}, u32[]{:S(2)}) copy-start(s32[512]{0:T(512)} %param.10) | copy-start | bytes 6148
  3.5 0.7 %copy-start.5 = (f32[4,8]{1,0:T(4,128)S(1)}, f32[4,8]{1,0:T(4,128)}, u32[]{:S(2)}) copy-start(f32[4,8]{1,0:T(4,128)} %coef_ref.1) | copy-start | bytes 388

commit v2 on v1

--- a/solution.py
+++ b/solution.py
@@ -12,7 +12,6 @@
 force_gain = 40.0
 LANES = 128
 PIECES = 3
-GROUP = 2
 f32 = jnp.float32
 bf16 = jnp.bfloat16
 
@@ -123,20 +122,41 @@
     targets = ttri_ref.shape[1]
     per_dev = coef_ref.shape[1]
     chips = n_dev // 2
-
-    def partner(step, sign):
-        chip = lax.rem(me // 2 + sign * (step // 2) + chips, chips)
-        return chip * 2 + lax.rem(me + step, 2)
+    inner = 1 << (chips.bit_length() - 1) // 2
+    outer = chips // inner
+    core = lax.rem(me, 2)
+    sibling = me + 1 - 2 * core
+    row_at = lax.rem(me // 2, inner)
+    column_at = me // (2 * inner)
+
+    def block_of(step):
+        o = lax.rem(column_at - lax.rem(step, outer) + outer, outer)
+        i = lax.rem(row_at - step // outer + inner, inner)
+        return (o * inner + i) * 2 + core
+
+    def outer_peer(step):
+        return (lax.rem(column_at + step, outer) * inner + row_at) * 2 + core
+
+    def inner_peer(step):
+        return (column_at * inner + lax.rem(row_at + step, inner)) * 2 + core
 
     barrier = pltpu.get_barrier_semaphore()
 
-    def greet(step, _):
+    def greet(device):
         pl.semaphore_signal(
-            barrier, inc=1, device_id={"blk": partner(step, 1)}, device_id_type=pl.DeviceIdType.MESH
+            barrier, inc=1, device_id={"blk": device}, device_id_type=pl.DeviceIdType.MESH
         )
-        return 0
-
-    lax.fori_loop(1, n_dev, greet, 0)
+
+    def each(low, high, act):
+        def body(step, _):
+            act(step)
+            return 0
+
+        lax.fori_loop(low, high, body, 0)
+
+    greet(sibling)
+    each(1, outer, lambda j: greet(outer_peer(j)))
+    each(1, inner, lambda j: greet(inner_peer(j)))
 
     index[...] = jnp.zeros_like(index)
     index[0:3, :] = stri_ref[...]
@@ -159,35 +179,41 @@
         held[me, t : t + 1, width : width + LANES] = disp_ref[2:3, t * LANES : (t + 1) * LANES]
     held[me, :, width + LANES : width + 2 * LANES] = spread
 
-    def copy(step):
+    def copy(source, device, sem):
         return pltpu.make_async_remote_copy(
-            src_ref=held.at[me],
-            dst_ref=held.at[me],
-            send_sem=send_sem.at[step],
-            recv_sem=recv_sem.at[me],
-            device_id={"blk": partner(step, 1)},
+            src_ref=held.at[source],
+            dst_ref=held.at[source],
+            send_sem=send_sem.at[sem],
+            recv_sem=recv_sem.at[source],
+            device_id={"blk": device},
             device_id_type=pl.DeviceIdType.MESH,
         )
 
-    def arrived(step):
-        source = partner(step, -1)
-        pltpu.make_async_remote_copy(
-            src_ref=held.at[source],
-            dst_ref=held.at[source],
-            send_sem=send_sem.at[step],
-            recv_sem=recv_sem.at[source],
-            device_id={"blk": source},
-            device_id_type=pl.DeviceIdType.MESH,
-        ).wait_recv()
-        return source
-
-    pl.semaphore_wait(barrier, n_dev - 1)
-
-    def send(step, _):
-        copy(step).start()
-        return 0
-
-    lax.fori_loop(1, n_dev, send, 0)
+    def to_sibling(step):
+        return copy(block_of(step), sibling, step)
+
+    def to_inner(step, j):
+        return copy(block_of(step), inner_peer(j), chips + step * inner + j)
+
+    def to_outer(j):
+        return copy(me, outer_peer(j), 2 * chips + j)
+
+    def arrived(source):
+        copy(source, sibling, 0).wait_recv()
+
+    def pass_on(step):
+        arrived(block_of(step))
+        to_sibling(step).start()
+
+    def pass_column(step):
+        arrived(block_of(step))
+        each(1, inner, lambda j: to_inner(step, j).start())
+        to_sibling(step).start()
+
+    pl.semaphore_wait(barrier, outer + inner - 1)
+    each(1, outer, lambda j: to_outer(j).start())
+    each(1, inner, lambda j: to_inner(0, j).start())
+    to_sibling(0).start()
 
     corner = [c[:, 0:targets] for c in corner]
     points, normals = triangles(corner, 3)
@@ -212,14 +238,23 @@
             jnp.concatenate(left, axis=1), jnp.concatenate(right, axis=0), preferred_element_type=f32
         )
 
-    arrived(1)
-    add_blocks([me, partner(1, -1)])
-
-    def step_blocks(step, _):
-        add_blocks([arrived(GROUP * step + g) for g in range(GROUP)])
-        return 0
-
-    lax.fori_loop(1, n_dev // GROUP, step_blocks, 0)
+    def add_chip(step):
+        own = block_of(step)
+        other = own + 1 - 2 * core
+        arrived(other)
+        add_blocks([own, other])
+
+    add_chip(0)
+    each(1, outer, pass_column)
+    ahead = min(outer + 1, chips)
+    each(outer, ahead, pass_on)
+
+    def pass_and_add(step):
+        pass_on(step + ahead - 1)
+        add_chip(step)
+
+    each(1, chips - ahead + 1, pass_and_add)
+    each(chips - ahead + 1, chips, add_chip)
 
     total = sums[0:48, :]
     for piece in range(1, PIECES):
@@ -251,11 +286,9 @@
     for m in range(3):
         out_ref[m : m + 1, :] = gain * influence[m] - pressure * normals[m]
 
-    def sent(step, _):
-        copy(step).wait_send()
-        return 0
-
-    lax.fori_loop(1, n_dev, sent, 0)
+    each(1, outer, lambda j: to_outer(j).wait_send())
+    each(0, outer, lambda step: each(1, inner, lambda j: to_inner(step, j).wait_send()))
+    each(0, chips, lambda step: to_sibling(step).wait_send())
 
 
 def solution(mesh):
@@ -275,7 +308,7 @@
                 pltpu.VMEM((8, LANES), f32),
                 pltpu.VMEM((80, targets), bf16),
                 pltpu.VMEM((48 * PIECES, targets), f32),
-                pltpu.SemaphoreType.DMA((n_dev,)),
+                pltpu.SemaphoreType.DMA((2 * n_dev,)),
                 pltpu.SemaphoreType.DMA((n_dev,)),
             ],
             compiler_params=pltpu.CompilerParams(

time: 31.7 us -> 29.3 us (0.924)
  the two profiles are of different devices: /device:TPU:27 before, /device:TPU:0 now
where the time goes in v2:
time: 29.3 us; the launch traced here: 28.8 us
  Pallas kernels  24 us (82%)
  local copies, waits for them, and re-layouts  4.79 us (16%)
    pallas_call x1, Pallas kernels, local(): pl.pallas_call(functools.partial(kernel, n_dev), out_shape=jax.ShapeDtype...  24 us
    unnamed x13, local copies, waits for them, and re-layouts  4.79 us

profile of v2, /device:TPU:0, one launch (start us, length us, event | category | flops | bytes accessed | tf_op | source)
XLA Modules:
  0.0 28.8 jit_solution(3139602980111691641)
XLA Ops:
  0.0 0.0 copy-start
  0.0 0.7 %copy-done = s32[3,1024]{1,0:T(4,128)S(1)} copy-done((s32[3,1024]{1,0:T(4,128)S(1)}, s32[3,1024]{1,0:T(4,128)}, u32[]{:S(2)}) %copy-start) | copy-done | bytes 12312
  0.7 0.0 copy-start.1
  0.7 0.7 %copy-done.1 = f32[3,1024]{1,0:T(4,128)S(1)} copy-done((f32[3,1024]{1,0:T(4,128)S(1)}, f32[3,1024]{1,0:T(4,128)}, u32[]{:S(2)}) %copy-start.1) | copy-done | bytes 12312
  1.4 0.0 copy-start.2
  1.4 0.7 %copy-done.2 = f32[3,512]{1,0:T(4,128)S(1)} copy-done((f32[3,512]{1,0:T(4,128)S(1)}, f32[3,512]{1,0:T(4,128)}, u32[]{:S(2)}) %copy-start.2) | copy-done | bytes 6168
  2.1 0.0 copy-start.3
  2.1 0.7 %copy-done.3 = s32[3,512]{1,0:T(4,128)S(1)} copy-done((s32[3,512]{1,0:T(4,128)S(1)}, s32[3,512]{1,0:T(4,128)}, u32[]{:S(2)}) %copy-start.3) | copy-done | bytes 6168
  2.8 0.0 copy-start.4
  2.8 0.7 %copy-done.4 = s32[512]{0:T(512)S(1)} copy-done((s32[512]{0:T(512)S(1)}, s32[512]{0:T(512)}, u32[]{:S(2)}) %copy-start.4) | copy-done | bytes 2072
  3.5 0.0 copy-start.5
  3.5 0.7 %copy-done.5 = f32[4,8]{1,0:T(4,128)S(1)} copy-done((f32[4,8]{1,0:T(4,128)S(1)}, f32[4,8]{1,0:T(4,128)}, u32[]{:S(2)}) %copy-start.5) | copy-done | bytes 152
  4.2 24.0 %shard_map.64 = f32[3,512]{1,0:T(4,128)S(1)} custom-call(f32[3,512]{1,0:T(4,128)S(1)} %copy-done.2, s32[3,1024]{1,0:T(4,128)S(1)} %copy-done, f32[3,1024]{1,0:T(4,128)S(1)} %copy-done.1, s32[3,512]{1,0:T(4,128)S(1)} %copy-done.3, s32[1,512]{1,0:T(1,128)S(1)} %bitcast.1, f32[4,8]{1,0:T(4,128)S(1)} %copy-done.5), custom_call_target="tpu_custom_call" | custom-call | tf_op jit(solution)/shard_map/pallas_call | solution.py:300
  28.2 0.6 %copy.8 = f32[3,512]{1,0:T(4,128)} copy(f32[3,512]{1,0:T(4,128)S(1)} %shard_map.64) | data formatting | bytes 12288
Async XLA Ops:
  0.0 0.7 %copy-start = (s32[3,1024]{1,0:T(4,128)S(1)}, s32[3,1024]{1,0:T(4,128)}, u32[]{:S(2)}) copy-start(s32[3,1024]{1,0:T(4,128)} %stri_ref.1) | copy-start | bytes 36868
  0.7 0.7 %copy-start.1 = (f32[3,1024]{1,0:T(4,128)S(1)}, f32[3,1024]{1,0:T(4,128)}, u32[]{:S(2)}) copy-start(f32[3,1024]{1,0:T(4,128)} %disp_ref.1) | copy-start | bytes 36868
  1.4 0.7 %copy-start.2 = (f32[3,512]{1,0:T(4,128)S(1)}, f32[3,512]{1,0:T(4,128)}, u32[]{:S(2)}) copy-start(f32[3,512]{1,0:T(4,128)} %vert_ref.1) | copy-start | bytes 18436
  2.1 0.7 %copy-start.3 = (s32[3,512]{1,0:T(4,128)S(1)}, s32[3,512]{1,0:T(4,128)}, u32[]{:S(2)}) copy-start(s32[3,512]{1,0:T(4,128)} %ttri_ref.1) | copy-start | bytes 18436
  2.8 0.7 %copy-start.4 = (s32[512]{0:T(512)S(1)}, s32[512]{0:T(512)}, u32[]{:S(2)}) copy-start(s32[512]{0:T(512)} %param.10) | copy-start | bytes 6148
  3.5 0.7 %copy-start.5 = (f32[4,8]{1,0:T(4,128)S(1)}, f32[4,8]{1,0:T(4,128)}, u32[]{:S(2)}) copy-start(f32[4,8]{1,0:T(4,128)} %coef_ref.1) | copy-start | bytes 388

commit v3 on v2

--- a/solution.py
+++ b/solution.py
@@ -29,7 +29,7 @@
     columns = []
     for t in range(index.shape[1] // LANES):
         where = index[:, t * LANES : (t + 1) * LANES]
-        low, high = where % LANES, where // LANES
+        low, high = where & (LANES - 1), where >> 7
         got = None
         for c in range(table.shape[1] // LANES):
             part = jnp.broadcast_to(table[:, c * LANES : (c + 1) * LANES], (8, LANES))
@@ -114,9 +114,17 @@
 
 
 def kernel(
-    n_dev, vert_ref, stri_ref, disp_ref, ttri_ref, frac_ref, coef_ref, out_ref,
-    held, index, coef, near_t, sums, send_sem, recv_sem,
+    n_dev, vert_in, stri_in, disp_in, ttri_in, frac_in, coef_in, out_ref,
+    vert_ref, stri_ref, disp_ref, ttri_ref, frac_ref, coef_ref,
+    held, index, coef, near_t, sums, load_sem, send_sem, recv_sem,
 ):
+    pairs = [
+        (vert_in, vert_ref), (stri_in, stri_ref), (ttri_in, ttri_ref),
+        (disp_in, disp_ref), (coef_in, coef_ref), (frac_in, frac_ref),
+    ]
+    loads = [pltpu.make_async_copy(src, dst, load_sem.at[k]) for k, (src, dst) in enumerate(pairs)]
+    for load in loads:
+        load.start()
     me = lax.axis_index("blk")
     width = stri_ref.shape[1]
     targets = ttri_ref.shape[1]
@@ -159,6 +167,8 @@
     each(1, inner, lambda j: greet(inner_peer(j)))
 
     index[...] = jnp.zeros_like(index)
+    for load in loads:
+        load.wait()
     index[0:3, :] = stri_ref[...]
     index[3:6, 0:targets] = ttri_ref[...]
     spots = index[...]
@@ -263,7 +273,7 @@
 
     tables = -(-n_dev * per_dev // LANES)
     which = jnp.broadcast_to(frac_ref[...], (8, targets))
-    low, high = which % LANES, which // LANES
+    low, high = which & (LANES - 1), which >> 7
     picked = jnp.zeros((8, targets), f32)
     for g in range(tables):
         table = jnp.zeros((8, LANES), f32)
@@ -297,24 +307,27 @@
     def local(vertices, source_tri, source_disp, target_tri, fracture_of, pressure_coeffs):
         width, targets = source_tri.shape[1], target_tri.shape[1]
         vmem = pl.BlockSpec(memory_space=pltpu.VMEM)
+        args = (vertices, source_tri, source_disp, target_tri, fracture_of[None, :], pressure_coeffs)
         return pl.pallas_call(
             functools.partial(kernel, n_dev),
             out_shape=jax.ShapeDtypeStruct((3, targets), f32),
-            in_specs=[vmem] * 6,
+            in_specs=[pl.BlockSpec(memory_space=pl.ANY)] * 6,
             out_specs=vmem,
-            scratch_shapes=[
+            scratch_shapes=[pltpu.VMEM(a.shape, a.dtype) for a in args]
+            + [
                 pltpu.VMEM((n_dev, 8, width + 2 * LANES), f32),
                 pltpu.VMEM((8, width), jnp.int32),
                 pltpu.VMEM((8, LANES), f32),
                 pltpu.VMEM((80, targets), bf16),
                 pltpu.VMEM((48 * PIECES, targets), f32),
+                pltpu.SemaphoreType.DMA((6,)),
                 pltpu.SemaphoreType.DMA((2 * n_dev,)),
                 pltpu.SemaphoreType.DMA((n_dev,)),
             ],
             compiler_params=pltpu.CompilerParams(
-                collective_id=0, has_side_effects=True, vmem_limit_bytes=48 << 20
+                collective_id=0, has_side_effects=True, vmem_limit_bytes=64 << 20
             ),
-        )(vertices, source_tri, source_disp, target_tri, fracture_of[None, :], pressure_coeffs)
+        )(*args)
 
     both = ("groups", "blk")
     wide = P(None, both)

time: 29.3 us -> 26.5 us (0.904)
  local copies, waits for them, and re-layouts: 4.79 us -> 1.3 us
  Pallas kernels: 24 us -> 24.9 us
    unnamed x13 -> x1, local copies, waits for them, and re-layouts: 4.79 us -> 1.3 us
    pallas_call x1, Pallas kernels: 24 us -> 24.9 us  [local(): pl.pallas_call(functools.partial(kernel, n_dev), out_shape=jax.ShapeDtype...]
where the time goes in v3:
time: 26.5 us; the launch traced here: 26.2 us
  Pallas kernels  24.9 us (94%)
  local copies, waits for them, and re-layouts  1.3 us (5%)
    pallas_call x1, Pallas kernels, local(): pl.pallas_call(functools.partial(kernel, n_dev), out_shape=jax.ShapeDtype...  24.9 us
    unnamed x1, local copies, waits for them, and re-layouts  1.3 us

profile of v3, /device:TPU:0, one launch (start us, length us, event | category | flops | bytes accessed | tf_op | source)
XLA Modules:
  0.0 26.2 jit_solution(2788432719822610157)
XLA Ops:
  0.0 24.9 %shard_map.64 = f32[3,512]{1,0:T(4,128)} custom-call(f32[3,512]{1,0:T(4,128)} %vert_in.1, s32[3,1024]{1,0:T(4,128)} %stri_in.1, f32[3,1024]{1,0:T(4,128)} %disp_in.1, s32[3,512]{1,0:T(4,128)} %ttri_in.1, s32[1,512]{1,0:T(1,128)} %bitcast.1, f32[4,8]{1,0:T(4,128)} %coef_in.1), custom_call_target="tpu_custom_call" | custom-call | tf_op jit(solution)/shard_map/pallas_call | solution.py:311
  24.9 1.3 %copy.8 = f32[3,512]{1,0:T(4,128)} copy(f32[3,512]{1,0:T(4,128)} %shard_map.64) | data formatting | bytes 12288
